TPU v7x, 32 devices: a whole 2x2x4 slice. The times are simulated.
32 devices in a mesh: graph: 8 (over z, x), rep: 4 (over y, core).
Axes of the slice: x: 2, y: 2, z: 4, core: 2. Of those that a mesh axis runs over, the one named last changes fastest.
Arguments:
- node_feats: bfloat16 [4, 128, 49, 256], P('rep', 'graph'), may hold values from -6 to 6
- species: int32 [4, 128], P('rep', 'graph'), may hold values from 0 to 89
- charge: int32 [4], P('rep'), may hold values from 0 to 8
- species_table: float32 [90, 256], replicated, may hold values from -6 to 6
- charge_table: float32 [9, 256], replicated, may hold values from -6 to 6
- so2_weight: bfloat16 [1792, 1792], replicated, may hold values from -0.125 to 0.125
- edge_frame: bfloat16 [4, 49, 2048], P('rep', None, 'graph'), as said below
- edge_src: int32 [4, 2048], P('rep', 'graph'), may hold values from 0 to 127, as said below
- edge_dst: int32 [4, 2048], P('rep', 'graph'), may hold values from 0 to 127, as said below
- edge_count: int32 [4, 8], P('rep', 'graph'), may hold values from 32 to 192, as said below
- out_cotangent: bfloat16 [4, 128, 49, 256], P('rep', 'graph'), may hold values from -6 to 6
Outputs:
- updated_feats: bfloat16 [4, 128, 49, 256], P('rep', 'graph')
- feat_grad: bfloat16 [4, 128, 49, 256], P('rep', 'graph')
- weight_grad: float32 [3211264], P(('graph', 'rep'))
- species_grad: float32 [90, 256], replicated
- charge_grad: float32 [9, 256], replicated
Inputs may be any that keep to these rules, and one draw needn't show every extreme that they name: `edge_count`: live slots of one device per cell. Two devices whose graph indices differ by half the axis hold at most 256 live slots together; in every cell some device holds exactly 192. `edge_src`: in a live slot the source atom's device (index // 16) is at most 2 devices from the slot's device along graph, cyclically; a slot that is not live holds its device's first atom. `edge_dst`: each slot's destination atom belongs to the device that holds the slot; a slot that is not live holds its device's first atom. `edge_frame`: for every edge and degree l the 2l+1 entries of degree l have unit sum of squares; the degree-0 entry is 1.
All inputs are finite; a program needn't handle non-finite values.
Results may differ from a plain program's by a relative error of at most 0.0066.
Values may be sent and summed in bfloat16 or wider, within the bound.
A program may use at most 128 MiB of HBM per device.

v0:
```python
import jax
import jax.numpy as jnp
from jax import lax
from jax.sharding import PartitionSpec as P

LMAX = 6
SPECIES = 90
CHARGES = 9
REACH = 2


MSG_SCALE = 0.25
PRECISE = lax.Precision.HIGHEST


def from_behind(block, axis, distance):
    devices = range(lax.axis_size(axis))
    route = [((i - distance) % len(devices), i) for i in devices]
    return lax.ppermute(block, axis, route)


def degree_spans():
    return [(degree * degree, (degree + 1) * (degree + 1)) for degree in range(LMAX + 1)]


def gate_forward(pre_act):
    return pre_act * jax.nn.sigmoid(pre_act[:, :1, :])


def gate_backward(pre_act, grad_out):
    sig_gate = jax.nn.sigmoid(pre_act[:, :1, :])
    cross_term = jnp.sum(grad_out * pre_act, axis=1, keepdims=True) * sig_gate * (1.0 - sig_gate)
    scaled = grad_out * sig_gate
    return jnp.concatenate([scaled[:, :1, :] + cross_term, scaled[:, 1:, :]], axis=1)


def gate_rows(pre_act):
    row_count = pre_act.shape[0]
    return gate_forward(pre_act.reshape(row_count, LMAX + 1, -1)).reshape(row_count, -1)


def gate_rows_back(pre_act, grad_out):
    row_count = pre_act.shape[0]
    shaped = gate_backward(
        pre_act.reshape(row_count, LMAX + 1, -1), grad_out.reshape(row_count, LMAX + 1, -1)
    )
    return shaped.reshape(row_count, -1)


def contract_rows(left_mat, right_mat):
    return lax.dot_general(
        left_mat, right_mat, (((0,), (0,)), ((), ())), preferred_element_type=jnp.float32
    )


def edge_coefs(onehot, frame_rows):
    return (onehot[:, :, None] * jnp.transpose(frame_rows)[:, None, :]).reshape(onehot.shape[0], -1)


def local(
    node_feats,
    species,
    charge,
    species_table,
    charge_table,
    so2_weight,
    edge_frame,
    edge_src,
    edge_dst,
    edge_count,
    out_cotangent,
):
    atoms_here = node_feats.shape[1]
    coef_count = node_feats.shape[2]
    channels = node_feats.shape[3]
    edges_here = edge_src.shape[1]
    graph_size = lax.axis_size("graph")
    graph_pos = lax.axis_index("graph")
    live_count = edge_count[0, 0]
    features = node_feats[0].astype(jnp.float32)
    spec_hot = (species[0][:, None] == jnp.arange(SPECIES, dtype=jnp.int32)[None, :]).astype(
        jnp.float32
    )
    charge_hot = (jnp.arange(CHARGES, dtype=jnp.int32) == charge[0]).astype(jnp.float32)
    embedding = (
        jnp.dot(spec_hot, species_table, precision=PRECISE)
        + jnp.dot(charge_hot, charge_table, precision=PRECISE)[None, :]
    )
    hidden = jnp.concatenate(
        [features[:, :1, :] + embedding[:, None, :], features[:, 1:, :]], axis=1
    ).astype(jnp.bfloat16)
    blocks = []
    for offset in range(-REACH, REACH + 1):
        if offset == 0:
            blocks.append(hidden)
        else:
            blocks.append(from_behind(hidden, "graph", -offset))
    block_total = len(blocks)
    nearby = jnp.stack(blocks, axis=0).reshape(block_total * atoms_here, coef_count, channels)
    sources = edge_src[0]
    targets = edge_dst[0]
    slot_ids = jnp.arange(edges_here, dtype=jnp.int32)
    live_mask = slot_ids < live_count
    rel_owner = (sources // atoms_here - graph_pos + REACH) % graph_size
    local_src = rel_owner * atoms_here + sources % atoms_here
    src_hot = (
        (local_src[:, None] == jnp.arange(block_total * atoms_here, dtype=jnp.int32)[None, :])
        & live_mask[:, None]
    ).astype(jnp.bfloat16)
    local_dst = targets - graph_pos * atoms_here
    dst_hot = (
        (local_dst[:, None] == jnp.arange(atoms_here, dtype=jnp.int32)[None, :])
        & live_mask[:, None]
    ).astype(jnp.bfloat16)
    frame_all = edge_frame[0]
    src_coefs = []
    dst_coefs = []
    rotated_pieces = []
    for lower_k, upper_k in degree_spans():
        frame_rows = frame_all[lower_k:upper_k]
        src_coef = edge_coefs(src_hot, frame_rows)
        src_coefs.append(src_coef)
        dst_coefs.append(edge_coefs(dst_hot, frame_rows))
        node_piece = nearby[:, lower_k:upper_k, :].reshape(-1, channels)
        rotated_pieces.append(jnp.dot(src_coef, node_piece, preferred_element_type=jnp.float32))
    rotated = jnp.concatenate(rotated_pieces, axis=1).astype(jnp.bfloat16)
    pre_act = jnp.dot(rotated, so2_weight, preferred_element_type=jnp.float32)
    gated = gate_rows(pre_act).astype(jnp.bfloat16)
    agg_pieces = []
    grad_pieces = []
    cotangent = out_cotangent[0]
    for degree, (lower_k, upper_k) in enumerate(degree_spans()):
        value_piece = gated[:, degree * channels : (degree + 1) * channels]
        agg_pieces.append(
            contract_rows(dst_coefs[degree], value_piece).reshape(
                atoms_here, upper_k - lower_k, channels
            )
        )
        cot_piece = cotangent[:, lower_k:upper_k, :].reshape(-1, channels)
        grad_pieces.append(
            MSG_SCALE * jnp.dot(dst_coefs[degree], cot_piece, preferred_element_type=jnp.float32)
        )
    aggregate = jnp.concatenate(agg_pieces, axis=1)
    updated = (features + MSG_SCALE * aggregate).astype(jnp.bfloat16)
    grad_values = jnp.concatenate(grad_pieces, axis=1)
    grad_pre = gate_rows_back(pre_act, grad_values).astype(jnp.bfloat16)
    weight_part = contract_rows(rotated, grad_pre)
    work_rot = lax.dot_general(
        grad_pre, so2_weight, (((1,), (1,)), ((), ())), preferred_element_type=jnp.float32
    ).astype(jnp.bfloat16)
    node_pieces = []
    for degree, (lower_k, upper_k) in enumerate(degree_spans()):
        rot_piece = work_rot[:, degree * channels : (degree + 1) * channels]
        node_pieces.append(
            contract_rows(src_coefs[degree], rot_piece).reshape(
                block_total * atoms_here, upper_k - lower_k, channels
            )
        )
    node_terms = (
        jnp.concatenate(node_pieces, axis=1)
        .astype(jnp.bfloat16)
        .reshape(block_total, atoms_here, coef_count, channels)
    )
    grad_total = jnp.zeros((atoms_here, coef_count, channels), jnp.float32)
    for offset in range(-REACH, REACH + 1):
        grad_piece = node_terms[offset + REACH]
        if offset == 0:
            grad_total = grad_total + grad_piece.astype(jnp.float32)
        else:
            grad_total = grad_total + from_behind(grad_piece, "graph", offset).astype(jnp.float32)
    feat_grad = (cotangent.astype(jnp.float32) + grad_total).astype(jnp.bfloat16)
    invariant = grad_total[:, 0, :]
    species_part = jnp.dot(jnp.transpose(spec_hot), invariant, precision=PRECISE)
    charge_part = charge_hot[:, None] * jnp.sum(invariant, axis=0)[None, :]
    species_grad, charge_grad = lax.psum((species_part, charge_part), ("graph", "rep"))
    flat_grad = weight_part.reshape(-1)
    weight_grad = lax.psum_scatter(flat_grad, ("graph", "rep"), scatter_dimension=0, tiled=True)
    return (updated[None], feat_grad[None], weight_grad, species_grad, charge_grad)


def solution(mesh):
    in_specs = (
        P("rep", "graph", None, None),
        P("rep", "graph"),
        P("rep"),
        P(),
        P(),
        P(),
        P("rep", None, "graph"),
        P("rep", "graph"),
        P("rep", "graph"),
        P("rep", "graph"),
        P("rep", "graph", None, None),
    )
    out_specs = (
        P("rep", "graph", None, None),
        P("rep", "graph", None, None),
        P(("graph", "rep")),
        P(),
        P(),
    )
    return jax.shard_map(local, mesh=mesh, in_specs=in_specs, out_specs=out_specs, check_vma=False)
```

profile of v0, /device:TPU:0, one launch (start us, length us, event | category | flops | bytes accessed | tf_op | source)
XLA Modules:
  0.0 348.7 jit_solution(5135623045955485624)
XLA Ops:
  8.0 1.1 convert_bitcast_fusion
  11.0 5.0 %collective-permute-start.3 = (bf16[16,49,256]{2,0,1:T(8,128)(2,1)}, bf16[16,49,256]{2,0,1:T(8,128)(2,1)}, u32[]{:S(2)}, u32[]{:S(2)}) collective-permute-start(bf16[16,49,256]{2,0,1:T(8,128)(2,1)} %pad_maximum_fusion.1), channel_id=1, source_target_pairs={{8,0},{12,4},{16,8},{20,12},{24,16},{28,20},{0,24},{4,28},{9,1},{1... | collective-permute-start | bytes 1204232 | tf_op jit(solution)/shard_map/ppermute | solution.py:19
  16.1 1.4 collective-permute-start.2
  31.0 1.1 fusion.7
  32.1 1.1 fusion.9
  33.2 1.1 fusion.11
  34.4 1.3 copy-done.3
  35.6 7.5 %collective-permute-done = bf16[16,49,256]{2,0,1:T(8,128)(2,1)} collective-permute-done((bf16[16,49,256]{2,0,1:T(8,128)(2,1)}, bf16[16,49,256]{2,0,1:T(8,128)(2,1)}, u32[]{:S(2)}, u32[]{:S(2)}) %collective-permute-start) | collective-permute-done | bytes 401440 | tf_op jit(solution)/shard_map/ppermute | solution.py:19
  43.1 1.0 bitcast_dynamic-update-slice_fusion.3
  44.1 1.2 bitcast_dynamic-update-slice_fusion.2
  45.4 1.2 bitcast_dynamic-update-slice_fusion.1
  46.5 1.0 bitcast_dynamic-update-slice_fusion
  50.4 3.1 fusion.131
  53.5 2.9 copy.52
  57.4 2.5 multiply_reduce_fusion
  60.1 1.0 fusion.58
  61.3 1.9 convolution_convert_fusion
  65.2 1.2 fusion.130
  66.4 3.2 collective-permute-start.4
  69.5 1.1 collective-permute-start.6
  70.6 3.6 %collective-permute-start.5 = (bf16[16,49,256]{2,0,1:T(8,128)(2,1)}, bf16[16,49,256]{2,0,1:T(8,128)(2,1)}, u32[]{:S(2)}, u32[]{:S(2)}) collective-permute-start(bf16[16,49,256]{2,0,1:T(8,128)(2,1)} %get-tuple-element.12), channel_id=1, source_target_pairs={{4,0},{8,4},{12,8},{16,12},{20,16},{24,20},{28,24},{0,28},{5,1},{9... | collective-permute-start | bytes 1204232 | tf_op jit(solution)/shard_map/ppermute | solution.py:19
  74.3 6.5 %fusion.132 = f32[1792,1792]{1,0:T(8,128)} fusion(bf16[256,1792]{0,1:T(8,128)(2,1)S(1)} %fusion.28, bf16[256,1792]{0,1:T(8,128)(2,1)S(1)} %bitcast.274), kind=kOutput, calls=%fused_computation.227 | convolution fusion | flops 1644167168 | bytes 14680064 | tf_op jit(solution)/shard_map/dot_general | solution.py:51
  80.8 13.6 %reshape.520 = f32[3211264]{0:T(1024)} reshape(f32[1792,1792]{1,0:T(8,128)} %fusion.132) | data formatting | bytes 25690112 | tf_op jit(solution)/shard_map/reshape | solution.py:176
  94.4 2.1 collective-permute-done.6
  96.5 2.4 fusion.51
  102.2 1.4 mul.342
  103.6 2.9 copy.53
  106.6 2.2 multiply_convert_fusion
  111.7 41.1 %psum.15 = f32[9,256]{1,0:T(8,128)} all-reduce(f32[9,256]{1,0:T(8,128)S(1)} %broadcast_multiply_fusion.16), channel_id=1, replica_groups=mesh['graph'=8,'rep'=4] {'graph','rep'}, use_global_device_ids=true, to_apply=%region_4.5 | all-reduce | flops 2304 | bytes 18432 | tf_op jit(solution)/shard_map/psum | solution.py:175
  152.8 185.7 %all-reduce.4.cloned.1.call-done = (f32[3211264]{0:T(1024)}, f32[90,256]{1,0:T(8,128)}) async-done(((f32[3211264]{0:T(1024)}, f32[90,256]{1,0:T(8,128)}), (f32[3211264]{0:T(1024)}, f32[90,256]{1,0:T(8,128)})) %all-reduce.4.cloned.1.call-update) | async-done | bytes 12937232
  338.5 1.8 dynamic-slice
  340.3 1.5 copy.152
  (183 shorter events, 26.4 us)
Async XLA Ops:
  7.2 2.8 copy-start
  7.2 2.8 copy-start.30
  7.2 11.8 %copy-start.25 = (bf16[1,49,256]{2,1,0:T(8,128)(2,1)S(1)}, bf16[1,49,256]{2,1,0:T(8,128)(2,1)}, u32[]{:S(2)}) copy-start(bf16[1,49,256]{2,1,0:T(8,128)(2,1)} %param.17) | copy-start | bytes 75268
  7.2 11.9 %copy-start.4 = (bf16[1,16,49,256]{3,1,2,0:T(8,128)(2,1)S(1)}, bf16[1,16,49,256]{3,1,2,0:T(8,128)(2,1)}, u32[]{:S(2)}) copy-start(bf16[1,16,49,256]{3,1,2,0:T(8,128)(2,1)} %param.21) | copy-start | bytes 1204228
  7.2 14.5 %copy-start.32 = (s32[1,256]{1,0:T(1,128)S(1)}, s32[1,256]{1,0:T(1,128)}, u32[]{:S(2)}) copy-start(s32[1,256]{1,0:T(1,128)} %param.18) | copy-start | bytes 3076
  7.2 14.5 %copy-start.33 = (s32[1,256]{1,0:T(1,128)S(1)}, s32[1,256]{1,0:T(1,128)}, u32[]{:S(2)}) copy-start(s32[1,256]{1,0:T(1,128)} %param.19) | copy-start | bytes 3076
  7.2 331.3 %all-reduce.4.cloned.1.call-start = ((), (), s32[]{:S(2)}) async-start(), calls=%async_computation | async-start | bytes 25886720
  11.0 35.5 %collective-permute-start.3 = (bf16[16,49,256]{2,0,1:T(8,128)(2,1)}, bf16[16,49,256]{2,0,1:T(8,128)(2,1)}, u32[]{:S(2)}, u32[]{:S(2)}) collective-permute-start(bf16[16,49,256]{2,0,1:T(8,128)(2,1)} %pad_maximum_fusion.1), channel_id=1, source_target_pairs={{8,0},{12,4},{16,8},{20,12},{24,16},{28,20},{0,24},{4,28},{9,1},{1... | collective-permute-start | bytes 1204232 | tf_op jit(solution)/shard_map/ppermute | solution.py:19
  16.1 29.3 %collective-permute-start.2 = (bf16[16,49,256]{2,0,1:T(8,128)(2,1)}, bf16[16,49,256]{2,0,1:T(8,128)(2,1)}, u32[]{:S(2)}, u32[]{:S(2)}) collective-permute-start(bf16[16,49,256]{2,0,1:T(8,128)(2,1)} %pad_maximum_fusion.1), channel_id=1, source_target_pairs={{4,0},{8,4},{12,8},{16,12},{20,16},{24,20},{28,24},{0,28},{5,1},{9... | collective-permute-start | bytes 1204232 | tf_op jit(solution)/shard_map/ppermute | solution.py:19
  17.4 26.7 %collective-permute-start.1 = (bf16[16,49,256]{2,0,1:T(8,128)(2,1)}, bf16[16,49,256]{2,0,1:T(8,128)(2,1)}, u32[]{:S(2)}, u32[]{:S(2)}) collective-permute-start(bf16[16,49,256]{2,0,1:T(8,128)(2,1)} %pad_maximum_fusion.1), channel_id=1, source_target_pairs={{28,0},{0,4},{4,8},{8,12},{12,16},{16,20},{20,24},{24,28},{29,1},{... | collective-permute-start | bytes 1204232 | tf_op jit(solution)/shard_map/ppermute | solution.py:19
  18.1 25.0 %collective-permute-start = (bf16[16,49,256]{2,0,1:T(8,128)(2,1)}, bf16[16,49,256]{2,0,1:T(8,128)(2,1)}, u32[]{:S(2)}, u32[]{:S(2)}) collective-permute-start(bf16[16,49,256]{2,0,1:T(8,128)(2,1)} %pad_maximum_fusion.1), channel_id=1, source_target_pairs={{24,0},{28,4},{0,8},{4,12},{8,16},{12,20},{16,24},{20,28},{25,1},{... | collective-permute-start | bytes 1204232 | tf_op jit(solution)/shard_map/ppermute | solution.py:19
  19.0 44.1 %copy-start.34 = (bf16[256]{0:T(256)(128)(2,1)}, bf16[256]{0:T(256)(128)(2,1)S(1)}, u32[]{:S(2)}) copy-start(bf16[256]{0:T(256)(128)(2,1)S(1)} %slice_reduce_fusion.1) | copy-start | bytes 1540
  19.1 13.0 %copy-start.23 = (bf16[256,11]{0,1:T(8,128)(2,1)}, bf16[256,11]{0,1:T(8,128)(2,1)S(1)}, u32[]{:S(2)}) copy-start(bf16[256,11]{0,1:T(8,128)(2,1)S(1)} %slice_bitcast_fusion.29) | copy-start | bytes 16900
  21.7 41.5 %copy-start.28 = (pred[256]{0:T(512)(128)(4,1)}, pred[256]{0:T(512)(128)(4,1)S(1)}, u32[]{:S(2)}) copy-start(pred[256]{0:T(512)(128)(4,1)S(1)} %iota_compare_fusion.5) | copy-start | bytes 772
  21.8 7.5 %copy-start.26 = (s32[1,256]{1,0:T(1,128)}, s32[1,256]{1,0:T(1,128)S(1)}, u32[]{:S(2)}) copy-start(s32[1,256]{1,0:T(1,128)S(1)} %broadcast_subtract_fusion) | copy-start | bytes 3076
  22.5 8.0 %copy-start.17 = (bf16[256,16,5]{0,2,1:T(8,128)(2,1)}, bf16[256,16,5]{0,2,1:T(8,128)(2,1)S(1)}, u32[]{:S(2)}) copy-start(bf16[256,16,5]{0,2,1:T(8,128)(2,1)S(1)} %broadcast_multiply_fusion.11) | copy-start | bytes 122884
  22.6 2.8 copy-start.7
  22.7 8.0 %copy-start.15 = (bf16[256,16,7]{0,2,1:T(8,128)(2,1)}, bf16[256,16,7]{0,2,1:T(8,128)(2,1)S(1)}, u32[]{:S(2)}) copy-start(bf16[256,16,7]{0,2,1:T(8,128)(2,1)S(1)} %broadcast_multiply_fusion.10) | copy-start | bytes 172036
  22.7 2.7 copy-start.9
  44.1 6.3 %slice-start = ((s8[6422528]{0:T(1024)(128)(4,1)}), s8[4194304]{0:T(1024)(128)(4,1)S(1)}, s32[]{:S(2)}) async-start(s8[6422528]{0:T(1024)(128)(4,1)} %bitcast.265), calls=%async_computation.1 | async-start | bytes 8388608
  47.6 2.8 slice-start.1
  53.5 7.7 %slice-start.2 = ((s8[6422528]{0:T(1024)(128)(4,1)}), s8[2228224]{0:T(1024)(128)(4,1)S(1)}, s32[]{:S(2)}) async-start(s8[6422528]{0:T(1024)(128)(4,1)} %bitcast.267), calls=%async_computation.3 | async-start | bytes 4456448
  57.4 3.8 %slice-start.3 = ((s8[6422528]{0:T(1024)(128)(4,1)}), s8[4194304]{0:T(1024)(128)(4,1)S(1)}, s32[]{:S(2)}) async-start(s8[6422528]{0:T(1024)(128)(4,1)} %bitcast.267), calls=%async_computation.4 | async-start | bytes 8388608
  61.2 2.6 copy-start.19
  66.4 28.0 %collective-permute-start.4 = (bf16[16,49,256]{2,0,1:T(8,128)(2,1)}, bf16[16,49,256]{2,0,1:T(8,128)(2,1)}, u32[]{:S(2)}, u32[]{:S(2)}) collective-permute-start(bf16[16,49,256]{2,0,1:T(8,128)(2,1)} %get-tuple-element.9), channel_id=1, source_target_pairs={{8,0},{12,4},{16,8},{20,12},{24,16},{28,20},{0,24},{4,28},{9,1},{1... | collective-permute-start | bytes 1204232 | tf_op jit(solution)/shard_map/ppermute | solution.py:19
  69.5 24.9 %collective-permute-start.7 = (bf16[16,49,256]{2,0,1:T(8,128)(2,1)}, bf16[16,49,256]{2,0,1:T(8,128)(2,1)}, u32[]{:S(2)}, u32[]{:S(2)}) collective-permute-start(bf16[16,49,256]{2,0,1:T(8,128)(2,1)} %get-tuple-element.10), channel_id=1, source_target_pairs={{24,0},{28,4},{0,8},{4,12},{8,16},{12,20},{16,24},{20,28},{25,1},{... | collective-permute-start | bytes 1204232 | tf_op jit(solution)/shard_map/ppermute | solution.py:19
  69.5 26.9 %collective-permute-start.6 = (bf16[16,49,256]{2,0,1:T(8,128)(2,1)}, bf16[16,49,256]{2,0,1:T(8,128)(2,1)}, u32[]{:S(2)}, u32[]{:S(2)}) collective-permute-start(bf16[16,49,256]{2,0,1:T(8,128)(2,1)} %get-tuple-element.11), channel_id=1, source_target_pairs={{28,0},{0,4},{4,8},{8,12},{12,16},{16,20},{20,24},{24,28},{29,1},{... | collective-permute-start | bytes 1204232 | tf_op jit(solution)/shard_map/ppermute | solution.py:19
  70.6 25.9 %collective-permute-start.5 = (bf16[16,49,256]{2,0,1:T(8,128)(2,1)}, bf16[16,49,256]{2,0,1:T(8,128)(2,1)}, u32[]{:S(2)}, u32[]{:S(2)}) collective-permute-start(bf16[16,49,256]{2,0,1:T(8,128)(2,1)} %get-tuple-element.12), channel_id=1, source_target_pairs={{4,0},{8,4},{12,8},{16,12},{20,16},{24,20},{28,24},{0,28},{5,1},{9... | collective-permute-start | bytes 1204232 | tf_op jit(solution)/shard_map/ppermute | solution.py:19
  80.8 15.7 %copy-start.5 = (bf16[1,16,49,256]{3,1,2,0:T(8,128)(2,1)S(1)}, bf16[1,16,49,256]{3,1,2,0:T(8,128)(2,1)}, u32[]{:S(2)}) copy-start(bf16[1,16,49,256]{3,1,2,0:T(8,128)(2,1)} %param.21) | copy-start | bytes 1204228
  94.4 5.4 %copy-start.31 = (s32[1,16]{1,0:T(1,128)S(1)}, s32[1,16]{1,0:T(1,128)}, u32[]{:S(2)}) copy-start(s32[1,16]{1,0:T(1,128)} %param.12) | copy-start | bytes 196
  103.6 2.9 copy-start.2
  109.2 232.6 %copy-start.1 = (f32[90,256]{1,0:T(8,128)S(1)}, f32[90,256]{1,0:T(8,128)}, u32[]{:S(2)}) copy-start(f32[90,256]{1,0:T(8,128)} %param.14) | copy-start | bytes 276484
  (17 other events, 24.2 us)
Sparse Core Ops, SparseCore 0:
  100.9 237.5 all-reduce.3
where the time goes:
time: 350 us; the launch traced here: 349 us
  waiting for transfers between devices  195 us (56%)
  local copies, waits for them, and re-layouts  42.3 us (12%)
  blocking collectives  41.1 us (12%)
  matrix products  23.6 us (7%)
  between operations  16.5 us (5%)
  starting transfers between devices  15.9 us (5%)
  other arithmetic  14 us (4%)
    unnamed x2, waiting for transfers between devices  186 us
    psum x1, blocking collectives, local(): lax.psum((species_part, charge_part), ('graph', 'rep'))  41.1 us
    ppermute x8, starting transfers between devices, from_behind(): return lax.ppermute(block, axis, route)  15.9 us
    reshape x1, local copies, waits for them, and re-layouts, local(): flat_grad = weight_part.reshape(-1)  13.6 us
    unnamed x85, local copies, waits for them, and re-layouts  10.4 us
    ppermute x8, waiting for transfers between devices, from_behind(): return lax.ppermute(block, axis, route)  9.54 us
    dot_general x15, matrix products, contract_rows(): lax.dot_general(left_mat, right_mat, (((0,), (0,)), ((), ())), preferred_...  9.33 us
  transfers between devices with their start and end apart: 9, of which 3 were waited for; matrix products, arithmetic and copies ran while one was open for 14% of the time, Pallas kernels for 0%

commit v1 on v0

v1 whole, which is shorter than its diff:
```python
import functools

import jax
import jax.numpy as jnp
from jax import lax
from jax.experimental import pallas as pl
from jax.experimental.pallas import tpu as pltpu
from jax.sharding import PartitionSpec as P

LMAX = 6
SPECIES = 90
CHARGES = 9
REACH = 2
NEAR = 2 * REACH + 1
MSG_SCALE = 0.25
PRECISE = lax.Precision.HIGHEST
MESH = pl.DeviceIdType.MESH
HOTS = 104
F32 = jnp.float32
BF16 = jnp.bfloat16
MIB = 1 << 20

OFFSETS = (-2, 2, -1, 1)


def degree_spans():
    return [(degree * degree, (degree + 1) * (degree + 1)) for degree in range(LMAX + 1)]


def dot_tn(left, right):
    return lax.dot_general(left, right, (((0,), (0,)), ((), ())), preferred_element_type=F32)


def dot_nn(left, right):
    return jnp.dot(left, right, preferred_element_type=F32)


def dot_nt(left, right):
    return lax.dot_general(left, right, (((1,), (1,)), ((), ())), preferred_element_type=F32)


def halo_kernel(size, feats_ref, spec_ref, charge_ref, stab_ref, ctab_ref, near_ref, hid, send_sem, recv_sem):
    atoms = feats_ref.shape[1]
    me = lax.axis_index("graph")
    rep = lax.axis_index("rep")
    barrier = pltpu.get_barrier_semaphore()
    for off in OFFSETS:
        pl.semaphore_signal(barrier, inc=1, device_id=(lax.rem(me + off + size, size), rep), device_id_type=MESH)
    spec_hot = (spec_ref[...] == lax.broadcasted_iota(jnp.int32, (atoms, SPECIES), 1)).astype(F32)
    charge_hot = (charge_ref[...] == lax.broadcasted_iota(jnp.int32, (atoms, CHARGES), 1)).astype(F32)
    embedding = jnp.dot(spec_hot, stab_ref[...], precision=PRECISE, preferred_element_type=F32) + jnp.dot(
        charge_hot, ctab_ref[...], precision=PRECISE, preferred_element_type=F32
    )
    hid[...] = feats_ref[...]
    hid[0] = (feats_ref[0].astype(F32) + embedding).astype(BF16)
    pl.semaphore_wait(barrier, len(OFFSETS))
    copies = []
    for i, off in enumerate(OFFSETS):
        slot = REACH - off
        copy = pltpu.make_async_remote_copy(
            src_ref=hid,
            dst_ref=near_ref.at[:, pl.ds(slot * atoms, atoms), :],
            send_sem=send_sem.at[i],
            recv_sem=recv_sem.at[i],
            device_id=(lax.rem(me + off + size, size), rep),
            device_id_type=MESH,
        )
        copy.start()
        copies.append(copy)
    near_ref[:, pl.ds(REACH * atoms, atoms), :] = hid[...]
    for copy in copies:
        copy.wait()


def compute_kernel(
    group_rows, pos_ref, near_ref, feats_ref, cot_ref, frame_ref, src_ref, dst_ref, w_ref,
    upd_ref, terms_ref, wp_ref, s_ref, d_ref, rot_ref, rott_ref, pre_ref, gv_ref, gp_ref, *rest,
):
    coef, near_atoms, ch = near_ref.shape
    atoms = feats_ref.shape[1]
    slots = src_ref.shape[1]
    me = pos_ref[0]
    live_count = pos_ref[1]
    size = pos_ref[2]
    live = lax.broadcasted_iota(jnp.int32, (1, slots), 1) < live_count
    sources = src_ref[...]
    rel = lax.rem(sources // atoms - me + REACH + size, size)
    local_src = jnp.where(live, rel * atoms + lax.rem(sources, atoms), -1)
    local_dst = jnp.where(live, dst_ref[...] - me * atoms, -1)
    s_hot = (lax.broadcasted_iota(jnp.int32, (near_atoms, slots), 0) == local_src).astype(F32)
    d_hot = (lax.broadcasted_iota(jnp.int32, (atoms, slots), 0) == local_dst).astype(F32)
    spans = degree_spans()
    for k in range(coef):
        row = frame_ref[pl.ds(k, 1), :]
        s_ref[k] = (s_hot * row).astype(BF16)
        d_ref[k] = (d_hot * row).astype(BF16)
    for l, (lo, hi) in enumerate(spans):
        cols = pl.ds(l * ch, ch)
        s_l = s_ref[lo:hi].reshape((hi - lo) * near_atoms, slots)
        rot = dot_tn(s_l, near_ref[lo:hi].reshape((hi - lo) * near_atoms, ch))
        rot_ref[:, cols] = rot.astype(BF16)
        rott_ref[cols, :] = jnp.transpose(rot).astype(BF16)
        d_l = d_ref[lo:hi].reshape((hi - lo) * atoms, slots)
        gv_ref[:, cols] = MSG_SCALE * dot_tn(d_l, cot_ref[lo:hi].reshape((hi - lo) * atoms, ch))

    def pre_body(l, carry):
        cols = pl.ds(pl.multiple_of(l * ch, ch), ch)
        pre_ref[:, cols] = dot_nn(rot_ref[...], w_ref[:, cols])
        return carry

    lax.fori_loop(0, LMAX + 1, pre_body, 0)
    sig = jax.nn.sigmoid(pre_ref[:, 0:ch])
    cross = jnp.zeros_like(sig)
    for l, (lo, hi) in enumerate(spans):
        cols = pl.ds(l * ch, ch)
        pre = pre_ref[:, cols]
        grad = gv_ref[:, cols]
        cross = cross + grad * pre
        values = (pre * sig).astype(BF16)
        d_l = d_ref[lo:hi].reshape((hi - lo) * atoms, slots)
        agg = dot_nn(d_l, values).reshape(hi - lo, atoms, ch)
        upd_ref[lo:hi] = (feats_ref[lo:hi].astype(F32) + MSG_SCALE * agg).astype(BF16)
        if l > 0:
            gp_ref[:, cols] = (grad * sig).astype(BF16)
    gp_ref[:, 0:ch] = (gv_ref[:, 0:ch] * sig + cross * sig * (1.0 - sig)).astype(BF16)

    for l, (lo, hi) in enumerate(spans):
        grad_rot = dot_nt(gp_ref[...], w_ref[pl.ds(l * ch, ch), :]).astype(BF16)
        s_l = s_ref[lo:hi].reshape((hi - lo) * near_atoms, slots)
        terms_ref[lo:hi] = dot_nn(s_l, grad_rot).astype(BF16).reshape(hi - lo, near_atoms, ch)

    if group_rows is None:

        def weight_flat(j, carry):
            cols = pl.ds(pl.multiple_of(j * ch, ch), ch)
            wp_ref[:, cols] = dot_nn(rott_ref[...], gp_ref[:, cols])
            return carry

        lax.fori_loop(0, LMAX + 1, weight_flat, 0)
        return
    wide_ref = rest[0]

    def weight_body(j, carry):
        cols = pl.ds(pl.multiple_of(j * ch, ch), ch)
        wide_ref[:, cols] = dot_nn(rott_ref[...], gp_ref[:, cols])
        return carry

    lax.fori_loop(0, LMAX + 1, weight_body, 0)
    half = wide_ref.shape[1] // 2

    def group_body(i, carry):
        rows = wide_ref[pl.ds(pl.multiple_of(i * group_rows, 8), group_rows), :]
        wp_ref[i] = jnp.concatenate([rows[:, :half], rows[:, half:]], axis=0).astype(BF16)
        return carry

    lax.fori_loop(0, wp_ref.shape[0], group_body, 0)


def bit_reversed(value, bits):
    return int(format(value, "0" + str(bits) + "b")[::-1], 2) if bits else 0


def stage_order(bits):
    return sorted(range(1 << bits), key=lambda t: -bit_reversed(t, bits))


def reduce_kernel(
    size, reps, bits, terms_ref, cot_ref, wp_ref, spec_ref, charge_ref,
    feat_ref, wg_ref, emb_ref,
    sent, got, near_got, emb_sent, emb_got, s_sem, r_sem, hs_sem, hr_sem, es_sem, er_sem,
):
    atoms = cot_ref.shape[1]
    me = lax.axis_index("graph")
    rep = lax.axis_index("rep")
    mine = me * reps + rep
    bit = [lax.rem(mine // (1 << b), 2) for b in range(bits)]

    def flipped(rel):
        total = 0
        for b in range(bits):
            total = total + (1 << b) * ((1 - bit[b]) if (rel >> b) & 1 else bit[b])
        return total

    def partner(b):
        other = flipped(1 << b)
        return (other // reps, lax.rem(other, reps))

    near_ids = [(lax.rem(me + off + size, size), rep) for off in OFFSETS]
    barrier = pltpu.get_barrier_semaphore()
    for device in near_ids + [partner(b) for b in range(bits)]:
        pl.semaphore_signal(barrier, inc=1, device_id=device, device_id_type=MESH)
    pl.semaphore_wait(barrier, len(near_ids) + bits)

    halo = []
    for i, off in enumerate(OFFSETS):
        copy = pltpu.make_async_remote_copy(
            src_ref=terms_ref.at[:, pl.ds((off + REACH) * atoms, atoms), :],
            dst_ref=near_got.at[i],
            send_sem=hs_sem.at[i],
            recv_sem=hr_sem.at[i],
            device_id=near_ids[i],
            device_id_type=MESH,
        )
        halo.append(copy)
    base = [sum(1 << (bits - 1 - q) for q in range(stage)) for stage in range(bits + 1)]
    copies = {}

    def launch(stage, t, source):
        slot = base[stage] + t
        copy = pltpu.make_async_remote_copy(
            src_ref=source,
            dst_ref=got.at[slot],
            send_sem=s_sem.at[slot],
            recv_sem=r_sem.at[slot],
            device_id=partner(stage),
            device_id_type=MESH,
        )
        copy.start()
        copies[stage, t] = copy

    for t in stage_order(bits - 1):
        launch(0, t, wp_ref.at[flipped(2 * t + 1)])
    for copy in halo:
        copy.start()

    def summed(stage, rel):
        total = wp_ref[flipped(rel)].astype(F32)
        for q in range(stage):
            total = total + got[base[q] + (rel >> (q + 1))].astype(F32)
        return total

    for stage in range(1, bits):
        for t in stage_order(bits - 1 - stage):
            rel = (2 * t + 1) << stage
            slot = base[stage] + t
            for q in range(stage):
                copies[q, rel >> (q + 1)].wait_recv()
            sent[slot - base[1]] = summed(stage, rel).astype(BF16)
            launch(stage, t, sent.at[slot - base[1]])

    for copy in halo:
        copy.wait_recv()
    grad = terms_ref[:, pl.ds(REACH * atoms, atoms), :].astype(F32)
    for i in range(len(OFFSETS)):
        grad = grad + near_got[i].astype(F32)
    feat_ref[...] = (cot_ref[...].astype(F32) + grad).astype(BF16)
    inv = grad[0]
    row_ids = lax.broadcasted_iota(jnp.int32, (HOTS, atoms), 0)
    hot = ((row_ids == spec_ref[...]) | (row_ids == SPECIES + charge_ref[...])).astype(F32)
    emb_ref[...] = jnp.dot(hot, inv, precision=PRECISE, preferred_element_type=F32)
    emb = []
    for b in range(bits):
        emb_sent[b] = emb_ref[...]
        copy = pltpu.make_async_remote_copy(
            src_ref=emb_sent.at[b],
            dst_ref=emb_got.at[b],
            send_sem=es_sem.at[b],
            recv_sem=er_sem.at[b],
            device_id=partner(b),
            device_id_type=MESH,
        )
        copy.start()
        copy.wait_recv()
        emb_ref[...] = emb_ref[...] + emb_got[b]
        emb.append(copy)

    for q in range(bits):
        copies[q, 0].wait_recv()
    total = summed(bits, 0)
    rows = wg_ref.shape[0] // 14
    for j in range(14):
        lanes = (j % 7) * 128
        part = (j // 7) * rows
        wg_ref[pl.ds(j, rows, stride=14), :] = total[part : part + rows, lanes : lanes + 128]
    for copy in list(copies.values()) + halo + emb:
        copy.wait_send()


def vmem(count):
    return [pl.BlockSpec(memory_space=pltpu.VMEM)] * count


def local(
    size, reps, node_feats, species, charge, species_table, charge_table, so2_weight,
    edge_frame, edge_src, edge_dst, edge_count, out_cotangent,
):
    _, atoms, coef, ch = node_feats.shape
    slots = edge_src.shape[1]
    feat = so2_weight.shape[0]
    devices = size * reps
    group_rows = feat // devices if feat % (devices * 8) == 0 and devices & (devices - 1) == 0 else None
    feats = jnp.transpose(node_feats[0], (1, 0, 2))
    cot = jnp.transpose(out_cotangent[0], (1, 0, 2))
    charge2 = charge.reshape(1, 1)
    near = pl.pallas_call(
        functools.partial(halo_kernel, size),
        out_shape=jax.ShapeDtypeStruct((coef, NEAR * atoms, ch), BF16),
        in_specs=vmem(5),
        out_specs=vmem(1)[0],
        scratch_shapes=[
            pltpu.VMEM((coef, atoms, ch), BF16),
            pltpu.SemaphoreType.DMA((len(OFFSETS),)),
            pltpu.SemaphoreType.DMA((len(OFFSETS),)),
        ],
        compiler_params=pltpu.CompilerParams(collective_id=0, has_side_effects=True, vmem_limit_bytes=32 * MIB),
    )(feats, species.reshape(atoms, 1), charge2, species_table, charge_table)

    pos = jnp.stack([lax.axis_index("graph").astype(jnp.int32), edge_count[0, 0], jnp.int32(size)])
    if group_rows is None:
        wp_shape = jax.ShapeDtypeStruct((feat, feat), F32)
        extra = []
    else:
        wp_shape = jax.ShapeDtypeStruct((devices, 2 * group_rows, feat // 2), BF16)
        extra = [pltpu.VMEM((feat, feat), F32)]
    upd, terms, wp = pl.pallas_call(
        functools.partial(compute_kernel, group_rows),
        out_shape=(
            jax.ShapeDtypeStruct((coef, atoms, ch), BF16),
            jax.ShapeDtypeStruct((coef, NEAR * atoms, ch), BF16),
            wp_shape,
        ),
        in_specs=[pl.BlockSpec(memory_space=pltpu.SMEM)] + vmem(7),
        out_specs=tuple(vmem(3)),
        scratch_shapes=[
            pltpu.VMEM((coef, NEAR * atoms, slots), BF16),
            pltpu.VMEM((coef, atoms, slots), BF16),
            pltpu.VMEM((slots, feat), BF16),
            pltpu.VMEM((feat, slots), BF16),
            pltpu.VMEM((slots, feat), F32),
            pltpu.VMEM((slots, feat), F32),
            pltpu.VMEM((slots, feat), BF16),
        ]
        + extra,
        compiler_params=pltpu.CompilerParams(vmem_limit_bytes=56 * MIB),
    )(pos, near, feats, cot, edge_frame[0].astype(F32), edge_src, edge_dst, so2_weight)

    if group_rows is None:
        return fallback(size, upd, terms, wp, cot, species, charge)
    bits = devices.bit_length() - 1
    feat_k, wg, emb = pl.pallas_call(
        functools.partial(reduce_kernel, size, reps, bits),
        out_shape=(
            jax.ShapeDtypeStruct((coef, atoms, ch), BF16),
            jax.ShapeDtypeStruct((feat * feat // devices // 128, 128), F32),
            jax.ShapeDtypeStruct((HOTS, ch), F32),
        ),
        in_specs=vmem(5),
        out_specs=tuple(vmem(3)),
        scratch_shapes=[
            pltpu.VMEM((devices // 2 - 1, 2 * group_rows, feat // 2), BF16),
            pltpu.VMEM((devices - 1, 2 * group_rows, feat // 2), BF16),
            pltpu.VMEM((len(OFFSETS), coef, atoms, ch), BF16),
            pltpu.VMEM((bits, HOTS, ch), F32),
            pltpu.VMEM((bits, HOTS, ch), F32),
            pltpu.SemaphoreType.DMA((devices - 1,)),
            pltpu.SemaphoreType.DMA((devices - 1,)),
            pltpu.SemaphoreType.DMA((len(OFFSETS),)),
            pltpu.SemaphoreType.DMA((len(OFFSETS),)),
            pltpu.SemaphoreType.DMA((bits,)),
            pltpu.SemaphoreType.DMA((bits,)),
        ],
        compiler_params=pltpu.CompilerParams(collective_id=1, has_side_effects=True, vmem_limit_bytes=48 * MIB),
    )(terms, cot, wp, species, charge2)
    return (
        jnp.transpose(upd, (1, 0, 2))[None],
        jnp.transpose(feat_k, (1, 0, 2))[None],
        wg.reshape(-1),
        emb[:SPECIES],
        emb[SPECIES : SPECIES + CHARGES],
    )


def fallback(size, upd, terms, wp, cot, species, charge):
    atoms = cot.shape[1]
    grad = jnp.zeros(cot.shape, F32)
    for off in range(-REACH, REACH + 1):
        piece = terms[:, (off + REACH) * atoms : (off + REACH + 1) * atoms, :]
        if off:
            piece = lax.ppermute(piece, "graph", [(i, (i + off) % size) for i in range(size)])
        grad = grad + piece.astype(F32)
    feat_k = (cot.astype(F32) + grad).astype(BF16)
    ids = jnp.arange(SPECIES + CHARGES, dtype=jnp.int32)[:, None]
    hot = ((ids == species) | (ids == SPECIES + charge[None, :])).astype(F32)
    emb = lax.psum(jnp.dot(hot, grad[0], precision=PRECISE), ("graph", "rep"))
    wg = lax.psum_scatter(wp.reshape(-1), ("graph", "rep"), scatter_dimension=0, tiled=True)
    return (
        jnp.transpose(upd, (1, 0, 2))[None],
        jnp.transpose(feat_k, (1, 0, 2))[None],
        wg,
        emb[:SPECIES],
        emb[SPECIES:],
    )


def solution(mesh):
    in_specs = (
        P("rep", "graph", None, None),
        P("rep", "graph"),
        P("rep"),
        P(),
        P(),
        P(),
        P("rep", None, "graph"),
        P("rep", "graph"),
        P("rep", "graph"),
        P("rep", "graph"),
        P("rep", "graph", None, None),
    )
    out_specs = (
        P("rep", "graph", None, None),
        P("rep", "graph", None, None),
        P(("graph", "rep")),
        P(),
        P(),
    )
    body = functools.partial(local, mesh.shape["graph"], mesh.shape["rep"])
    return jax.shard_map(body, mesh=mesh, in_specs=in_specs, out_specs=out_specs, check_vma=False)
```

time: 350 us -> 126 us (0.36)
  waiting for transfers between devices: 195 us -> 0 us
  Pallas kernels: 0 us -> 113 us
  blocking collectives: 41.1 us -> 0 us
  local copies, waits for them, and re-layouts: 42.3 us -> 8.98 us
  matrix products: 23.6 us -> 0 us
  starting transfers between devices: 15.9 us -> 0 us
  between operations: 16.5 us -> 1.99 us
  other arithmetic: 14 us -> 1.96 us
    unnamed x2 -> x0, waiting for transfers between devices: 186 us -> none
    pallas_call x0 -> x3, Pallas kernels: none -> 113 us  [the longest x1 59.5 us: local(): pl.pallas_call(functools.partial(reduce_kernel, size, reps, bits), out_sh...]
    psum x1 -> x0, blocking collectives: 41.1 us -> none  [local(): lax.psum((species_part, charge_part), ('graph', 'rep'))]
    dot_general x34 -> x0, matrix products: 23.6 us -> none  [the longest x15 9.33 us: contract_rows(): lax.dot_general(left_mat, right_mat, (((0,), (0,)), ((), ())), preferred_...]
    ppermute x8 -> x0, starting transfers between devices: 15.9 us -> none  [from_behind(): return lax.ppermute(block, axis, route)]
    reshape x1, local copies, waits for them, and re-layouts: 13.6 us -> 0.73 us  [local(): species.reshape(atoms, 1)]
    ppermute x8 -> x0, waiting for transfers between devices: 9.54 us -> none  [from_behind(): return lax.ppermute(block, axis, route)]
    dot_general x13 -> x0, local copies, waits for them, and re-layouts: 8.48 us -> none  [the longest x12 5.59 us: contract_rows(): lax.dot_general(left_mat, right_mat, (((0,), (0,)), ((), ())), preferred_...]
  transfers between devices with their start and end apart: 9 -> 0, of which waited for: 3 -> 0; matrix products, arithmetic and copies ran while one was open for 14% -> 0% of each run, Pallas kernels for 0% -> 0%
where the time goes in v1:
time: 126 us
  Pallas kernels  113 us (90%)
  local copies, waits for them, and re-layouts  8.98 us (7%)
  between operations  1.99 us (2%)
  other arithmetic  1.96 us (2%)
    pallas_call x1, Pallas kernels, local(): pl.pallas_call(functools.partial(reduce_kernel, size, reps, bits), out_sh...  59.5 us
    pallas_call x1, Pallas kernels, local(): pl.pallas_call(functools.partial(halo_kernel, size), out_shape=jax.ShapeD...  32.8 us
    pallas_call x1, Pallas kernels, local(): pl.pallas_call(functools.partial(compute_kernel, group_rows), out_shape=(...  20.6 us
    unnamed x16, local copies, waits for them, and re-layouts  6.99 us

profile of v1, /device:TPU:0, one launch (start us, length us, event | category | flops | bytes accessed | tf_op | source)
XLA Modules:
  0.0 125.8 jit_solution(6918137393882609537)
XLA Ops:
  0.6 0.0 copy-start.6
  1.9 0.6 pad_add_fusion.pos_ref
  2.5 0.7 copy.16.spec_ref
  3.3 1.4 %bitcast_convert_fusion.frame_ref = f32[49,256]{1,0:T(8,128)} fusion(bf16[1,49,256]{2,1,0:T(8,128)(2,1)} %param.17), kind=kLoop, calls=%fused_computation | loop fusion | flops 12544 | bytes 75264 | tf_op jit(solution)/shard_map/convert_element_type | solution.py:335
  4.6 0.0 copy-start.2
  4.6 1.0 copy-done.2
  5.6 0.0 copy-start.4
  5.6 0.9 copy-done.4
  6.5 0.0 copy-start.5
  6.5 0.7 copy-done.5
  7.3 0.0 copy-start.3
  7.3 32.8 %shard_map.146.near_ref = bf16[49,80,256]{2,1,0:T(8,128)(2,1)S(1)} custom-call(bf16[49,16,256]{2,1,0:T(8,128)(2,1)S(1)} %bitcast.24, s32[16,1]{1,0:T(8,128)S(1)} %copy.16.spec_ref, s32[1,1]{1,0:T(1,128)} %bitcast.20.charge_ref, f32[90,256]{1,0:T(8,128)S(1)} %copy-done.4, f32[9,256]{1,0:T(8,128)S(1)} %copy-done.5), custom_call_target="tpu_custom_call" | custom-call | tf_op jit(solution)/shard_map/pallas_call | solution.py:295
  40.1 0.0 copy-start
  40.1 1.3 %copy-done = bf16[49,80,256]{2,1,0:T(8,128)(2,1)} copy-done((bf16[49,80,256]{2,1,0:T(8,128)(2,1)}, bf16[49,80,256]{2,1,0:T(8,128)(2,1)S(1)}, u32[]{:S(2)}) %copy-start) | copy-done | bytes 2007064
  41.4 20.6 %shard_map.147 = (bf16[49,16,256]{2,1,0:T(8,128)(2,1)}, bf16[49,80,256]{2,1,0:T(8,128)(2,1)}, bf16[32,112,896]{2,1,0:T(8,128)(2,1)}) custom-call(s32[3]{0:T(128)} %pad_add_fusion.pos_ref, bf16[49,80,256]{2,1,0:T(8,128)(2,1)} %copy-done, bf16[49,16,256]{2,1,0:T(8,128)(2,1)} %bitcast.23, bf16[49,16,256]{2,1,0:T(8,128)(2,1)} %bitcast.25, ...), custom_call_target="tpu_custom_call" | custom-call | tf_op jit(solution)/shard_map/pallas_call | solution.py:315
  62.0 0.0 copy-done.6
  62.0 0.0 copy-done.3
  62.0 0.0 copy-start.1
  62.0 1.6 %copy-done.1 = bf16[49,80,256]{2,1,0:T(8,128)(2,1)S(1)} copy-done((bf16[49,80,256]{2,1,0:T(8,128)(2,1)S(1)}, bf16[49,80,256]{2,1,0:T(8,128)(2,1)}, u32[]{:S(2)}) %copy-start.1) | copy-done | bytes 2007064
  63.6 59.5 %shard_map.148 = (bf16[49,16,256]{2,1,0:T(8,128)(2,1)S(1)}, f32[784,128]{1,0:T(8,128)S(1)}, f32[104,256]{1,0:T(8,128)S(1)}) custom-call(bf16[49,80,256]{2,1,0:T(8,128)(2,1)S(1)} %copy-done.1, bf16[49,16,256]{2,1,0:T(8,128)(2,1)S(1)} %bitcast.26, bf16[32,112,896]{2,1,0:T(8,128)(2,1)} %get-tuple-element.13.wp_ref, s32[1,16]{1,0:T(1,128)S(1)} %copy-done.6, ...), custom_call_target="tpu_custom_call" | custom-call | tf_op jit(solution)/shard_map/pallas_call | solution.py:340
  123.0 0.6 slice.7
  123.7 0.6 slice.6
  124.3 0.7 copy.21
  125.1 0.8 copy.22
Async XLA Ops:
  0.6 61.4 %copy-start.6 = (s32[1,16]{1,0:T(1,128)S(1)}, s32[1,16]{1,0:T(1,128)}, u32[]{:S(2)}) copy-start(s32[1,16]{1,0:T(1,128)} %spec_ref.1) | copy-start | bytes 196
  4.6 1.0 copy-start.2
  5.6 0.9 copy-start.4
  6.5 0.7 copy-start.5
  7.3 54.8 %copy-start.3 = (bf16[1,16,49,256]{3,1,2,0:T(8,128)(2,1)S(1)}, bf16[1,16,49,256]{3,1,2,0:T(8,128)(2,1)}, u32[]{:S(2)}) copy-start(bf16[1,16,49,256]{3,1,2,0:T(8,128)(2,1)} %param.21) | copy-start | bytes 1204228
  40.1 1.3 %copy-start = (bf16[49,80,256]{2,1,0:T(8,128)(2,1)}, bf16[49,80,256]{2,1,0:T(8,128)(2,1)S(1)}, u32[]{:S(2)}) copy-start(bf16[49,80,256]{2,1,0:T(8,128)(2,1)S(1)} %shard_map.146.near_ref) | copy-start | bytes 6021124
  62.0 1.6 %copy-start.1 = (bf16[49,80,256]{2,1,0:T(8,128)(2,1)S(1)}, bf16[49,80,256]{2,1,0:T(8,128)(2,1)}, u32[]{:S(2)}) copy-start(bf16[49,80,256]{2,1,0:T(8,128)(2,1)} %get-tuple-element.12.terms_ref) | copy-start | bytes 6021124

commit v2 on v1

--- a/solution.py
+++ b/solution.py
@@ -43,9 +43,12 @@
     atoms = feats_ref.shape[1]
     me = lax.axis_index("graph")
     rep = lax.axis_index("rep")
+    odd = lax.rem(me, 2)
+    across = me + 1 - 2 * odd
+    above, below = lax.rem(me + 2, size), lax.rem(me + size - 2, size)
     barrier = pltpu.get_barrier_semaphore()
-    for off in OFFSETS:
-        pl.semaphore_signal(barrier, inc=1, device_id=(lax.rem(me + off + size, size), rep), device_id_type=MESH)
+    for other in (above, below, across):
+        pl.semaphore_signal(barrier, inc=1, device_id=(other, rep), device_id_type=MESH)
     spec_hot = (spec_ref[...] == lax.broadcasted_iota(jnp.int32, (atoms, SPECIES), 1)).astype(F32)
     charge_hot = (charge_ref[...] == lax.broadcasted_iota(jnp.int32, (atoms, CHARGES), 1)).astype(F32)
     embedding = jnp.dot(spec_hot, stab_ref[...], precision=PRECISE, preferred_element_type=F32) + jnp.dot(
@@ -53,23 +56,65 @@
     )
     hid[...] = feats_ref[...]
     hid[0] = (feats_ref[0].astype(F32) + embedding).astype(BF16)
-    pl.semaphore_wait(barrier, len(OFFSETS))
+    pl.semaphore_wait(barrier, 3)
+    chunks = send_sem.shape[1]
+    span = hid.shape[0] // chunks
+
+    def place(c, slot):
+        return near_ref.at[pl.ds(c * span, span), pl.ds(pl.multiple_of(slot * atoms, atoms), atoms), :]
+
+    def move(c, source, slot, kind, other):
+        return pltpu.make_async_remote_copy(
+            src_ref=source,
+            dst_ref=place(c, slot),
+            send_sem=send_sem.at[kind, c],
+            recv_sem=recv_sem.at[kind, c],
+            device_id=(other, rep),
+            device_id_type=MESH,
+        )
+
     copies = []
-    for i, off in enumerate(OFFSETS):
-        slot = REACH - off
-        copy = pltpu.make_async_remote_copy(
-            src_ref=hid,
-            dst_ref=near_ref.at[:, pl.ds(slot * atoms, atoms), :],
-            send_sem=send_sem.at[i],
-            recv_sem=recv_sem.at[i],
-            device_id=(lax.rem(me + off + size, size), rep),
-            device_id_type=MESH,
-        )
-        copy.start()
-        copies.append(copy)
+    for c in range(chunks):
+        own = hid.at[pl.ds(c * span, span)]
+        copies.append(
+            [
+                move(c, own, 2 * REACH, 0, below),
+                move(c, own, 0, 1, above),
+                move(c, own, 1 + 2 * odd, 2, across),
+            ]
+        )
+        for copy in copies[c]:
+            copy.start()
     near_ref[:, pl.ds(REACH * atoms, atoms), :] = hid[...]
-    for copy in copies:
-        copy.wait()
+    far = 2 * REACH * (1 - odd)
+    relays = []
+    for c in range(chunks):
+        arrived = pltpu.make_async_remote_copy(
+            src_ref=hid.at[pl.ds(c * span, span)],
+            dst_ref=place(c, far),
+            send_sem=send_sem.at[0, c],
+            recv_sem=recv_sem.at[odd, c],
+            device_id=(across, rep),
+            device_id_type=MESH,
+        )
+        arrived.wait_recv()
+        relay = move(c, place(c, far), 3 - 2 * odd, 3, across)
+        relay.start()
+        relays.append(relay)
+    for c in range(chunks):
+        other_way = pltpu.make_async_remote_copy(
+            src_ref=hid.at[pl.ds(c * span, span)],
+            dst_ref=place(c, 2 * REACH - far),
+            send_sem=send_sem.at[0, c],
+            recv_sem=recv_sem.at[1 - odd, c],
+            device_id=(across, rep),
+            device_id_type=MESH,
+        )
+        other_way.wait_recv()
+        copies[c][2].wait_recv()
+        relays[c].wait_recv()
+        for copy in copies[c] + [relays[c]]:
+            copy.wait_send()
 
 
 def compute_kernel(
@@ -229,7 +274,7 @@
             total = total + got[base[q] + (rel >> (q + 1))].astype(F32)
         return total
 
-    for stage in range(1, bits):
+    def advance(stage):
         for t in stage_order(bits - 1 - stage):
             rel = (2 * t + 1) << stage
             slot = base[stage] + t
@@ -238,18 +283,9 @@
             sent[slot - base[1]] = summed(stage, rel).astype(BF16)
             launch(stage, t, sent.at[slot - base[1]])
 
-    for copy in halo:
-        copy.wait_recv()
-    grad = terms_ref[:, pl.ds(REACH * atoms, atoms), :].astype(F32)
-    for i in range(len(OFFSETS)):
-        grad = grad + near_got[i].astype(F32)
-    feat_ref[...] = (cot_ref[...].astype(F32) + grad).astype(BF16)
-    inv = grad[0]
-    row_ids = lax.broadcasted_iota(jnp.int32, (HOTS, atoms), 0)
-    hot = ((row_ids == spec_ref[...]) | (row_ids == SPECIES + charge_ref[...])).astype(F32)
-    emb_ref[...] = jnp.dot(hot, inv, precision=PRECISE, preferred_element_type=F32)
     emb = []
-    for b in range(bits):
+
+    def emb_send(b):
         emb_sent[b] = emb_ref[...]
         copy = pltpu.make_async_remote_copy(
             src_ref=emb_sent.at[b],
@@ -260,9 +296,38 @@
             device_id_type=MESH,
         )
         copy.start()
-        copy.wait_recv()
+        emb.append(copy)
+
+    def emb_take(b):
+        emb[b].wait_recv()
         emb_ref[...] = emb_ref[...] + emb_got[b]
-        emb.append(copy)
+
+    def finish_nodes():
+        for copy in halo:
+            copy.wait_recv()
+        grad = terms_ref[:, pl.ds(REACH * atoms, atoms), :].astype(F32)
+        for i in range(len(OFFSETS)):
+            grad = grad + near_got[i].astype(F32)
+        feat_ref[...] = (cot_ref[...].astype(F32) + grad).astype(BF16)
+        row_ids = lax.broadcasted_iota(jnp.int32, (HOTS, atoms), 0)
+        hot = ((row_ids == spec_ref[...]) | (row_ids == SPECIES + charge_ref[...])).astype(F32)
+        emb_ref[...] = jnp.dot(hot, grad[0], precision=PRECISE, preferred_element_type=F32)
+
+    advance(1)
+    advance(2)
+    finish_nodes()
+    emb_send(0)
+    taken = 0
+    for stage in range(3, bits):
+        advance(stage)
+        emb_take(taken)
+        taken += 1
+        emb_send(taken)
+    while taken < bits:
+        emb_take(taken)
+        taken += 1
+        if taken < bits:
+            emb_send(taken)
 
     for q in range(bits):
         copies[q, 0].wait_recv()
@@ -292,6 +357,7 @@
     feats = jnp.transpose(node_feats[0], (1, 0, 2))
     cot = jnp.transpose(out_cotangent[0], (1, 0, 2))
     charge2 = charge.reshape(1, 1)
+    chunks = LMAX + 1 if coef % (LMAX + 1) == 0 else 1
     near = pl.pallas_call(
         functools.partial(halo_kernel, size),
         out_shape=jax.ShapeDtypeStruct((coef, NEAR * atoms, ch), BF16),
@@ -299,8 +365,8 @@
         out_specs=vmem(1)[0],
         scratch_shapes=[
             pltpu.VMEM((coef, atoms, ch), BF16),
-            pltpu.SemaphoreType.DMA((len(OFFSETS),)),
-            pltpu.SemaphoreType.DMA((len(OFFSETS),)),
+            pltpu.SemaphoreType.DMA((4, chunks)),
+            pltpu.SemaphoreType.DMA((4, chunks)),
         ],
         compiler_params=pltpu.CompilerParams(collective_id=0, has_side_effects=True, vmem_limit_bytes=32 * MIB),
     )(feats, species.reshape(atoms, 1), charge2, species_table, charge_table)

time: 126 us -> 122 us (0.968)
  Pallas kernels: 113 us -> 108 us
    pallas_call x1, Pallas kernels: 32.8 us -> 27.6 us  [local(): pl.pallas_call(functools.partial(halo_kernel, size), out_shape=jax.ShapeD...]
where the time goes in v2:
time: 122 us; the launch traced here: 121 us
  Pallas kernels  108 us (89%)
  local copies, waits for them, and re-layouts  8.98 us (7%)
  between operations  1.99 us (2%)
  other arithmetic  1.96 us (2%)
    pallas_call x1, Pallas kernels, local(): pl.pallas_call(functools.partial(reduce_kernel, size, reps, bits), out_sh...  60.1 us
    pallas_call x1, Pallas kernels, local(): pl.pallas_call(functools.partial(halo_kernel, size), out_shape=jax.ShapeD...  27.6 us
    pallas_call x1, Pallas kernels, local(): pl.pallas_call(functools.partial(compute_kernel, group_rows), out_shape=(...  20.6 us
    unnamed x16, local copies, waits for them, and re-layouts  6.99 us

profile of v2, /device:TPU:0, one launch (start us, length us, event | category | flops | bytes accessed | tf_op | source)
XLA Modules:
  0.0 121.2 jit_solution(6122544811318341380)
XLA Ops:
  0.6 0.0 copy-start.6
  1.9 0.6 pad_add_fusion.pos_ref
  2.5 0.7 copy.16.spec_ref
  3.3 1.4 %bitcast_convert_fusion.frame_ref = f32[49,256]{1,0:T(8,128)} fusion(bf16[1,49,256]{2,1,0:T(8,128)(2,1)} %param.17), kind=kLoop, calls=%fused_computation | loop fusion | flops 12544 | bytes 75264 | tf_op jit(solution)/shard_map/convert_element_type | solution.py:401
  4.6 0.0 copy-start.2
  4.6 1.0 copy-done.2
  5.6 0.0 copy-start.4
  5.6 0.9 copy-done.4
  6.5 0.0 copy-start.5
  6.5 0.7 copy-done.5
  7.3 0.0 copy-start.3
  7.3 27.6 %shard_map.146.near_ref = bf16[49,80,256]{2,1,0:T(8,128)(2,1)S(1)} custom-call(bf16[49,16,256]{2,1,0:T(8,128)(2,1)S(1)} %bitcast.24, s32[16,1]{1,0:T(8,128)S(1)} %copy.16.spec_ref, s32[1,1]{1,0:T(1,128)} %bitcast.20.charge_ref, f32[90,256]{1,0:T(8,128)S(1)} %copy-done.4, f32[9,256]{1,0:T(8,128)S(1)} %copy-done.5), custom_call_target="tpu_custom_call" | custom-call | tf_op jit(solution)/shard_map/pallas_call | solution.py:361
  34.9 0.0 copy-start
  34.9 1.3 %copy-done = bf16[49,80,256]{2,1,0:T(8,128)(2,1)} copy-done((bf16[49,80,256]{2,1,0:T(8,128)(2,1)}, bf16[49,80,256]{2,1,0:T(8,128)(2,1)S(1)}, u32[]{:S(2)}) %copy-start) | copy-done | bytes 2007064
  36.2 20.6 %shard_map.147 = (bf16[49,16,256]{2,1,0:T(8,128)(2,1)}, bf16[49,80,256]{2,1,0:T(8,128)(2,1)}, bf16[32,112,896]{2,1,0:T(8,128)(2,1)}) custom-call(s32[3]{0:T(128)} %pad_add_fusion.pos_ref, bf16[49,80,256]{2,1,0:T(8,128)(2,1)} %copy-done, bf16[49,16,256]{2,1,0:T(8,128)(2,1)} %bitcast.23, bf16[49,16,256]{2,1,0:T(8,128)(2,1)} %bitcast.25, ...), custom_call_target="tpu_custom_call" | custom-call | tf_op jit(solution)/shard_map/pallas_call | solution.py:381
  56.8 0.0 copy-done.6
  56.8 0.0 copy-done.3
  56.8 0.0 copy-start.1
  56.8 1.6 %copy-done.1 = bf16[49,80,256]{2,1,0:T(8,128)(2,1)S(1)} copy-done((bf16[49,80,256]{2,1,0:T(8,128)(2,1)S(1)}, bf16[49,80,256]{2,1,0:T(8,128)(2,1)}, u32[]{:S(2)}) %copy-start.1) | copy-done | bytes 2007064
  58.4 60.1 %shard_map.148 = (bf16[49,16,256]{2,1,0:T(8,128)(2,1)S(1)}, f32[784,128]{1,0:T(8,128)S(1)}, f32[104,256]{1,0:T(8,128)S(1)}) custom-call(bf16[49,80,256]{2,1,0:T(8,128)(2,1)S(1)} %copy-done.1, bf16[49,16,256]{2,1,0:T(8,128)(2,1)S(1)} %bitcast.26, bf16[32,112,896]{2,1,0:T(8,128)(2,1)} %get-tuple-element.13.wp_ref, s32[1,16]{1,0:T(1,128)S(1)} %copy-done.6, ...), custom_call_target="tpu_custom_call" | custom-call | tf_op jit(solution)/shard_map/pallas_call | solution.py:406
  118.5 0.6 slice.7
  119.1 0.6 slice.6
  119.7 0.7 copy.21
  120.5 0.8 copy.22
Async XLA Ops:
  0.6 56.2 %copy-start.6 = (s32[1,16]{1,0:T(1,128)S(1)}, s32[1,16]{1,0:T(1,128)}, u32[]{:S(2)}) copy-start(s32[1,16]{1,0:T(1,128)} %spec_ref.1) | copy-start | bytes 196
  4.6 1.0 copy-start.2
  5.6 0.9 copy-start.4
  6.5 0.7 copy-start.5
  7.3 49.6 %copy-start.3 = (bf16[1,16,49,256]{3,1,2,0:T(8,128)(2,1)S(1)}, bf16[1,16,49,256]{3,1,2,0:T(8,128)(2,1)}, u32[]{:S(2)}) copy-start(bf16[1,16,49,256]{3,1,2,0:T(8,128)(2,1)} %param.21) | copy-start | bytes 1204228
  34.9 1.3 %copy-start = (bf16[49,80,256]{2,1,0:T(8,128)(2,1)}, bf16[49,80,256]{2,1,0:T(8,128)(2,1)S(1)}, u32[]{:S(2)}) copy-start(bf16[49,80,256]{2,1,0:T(8,128)(2,1)S(1)} %shard_map.146.near_ref) | copy-start | bytes 6021124
  56.8 1.6 %copy-start.1 = (bf16[49,80,256]{2,1,0:T(8,128)(2,1)S(1)}, bf16[49,80,256]{2,1,0:T(8,128)(2,1)}, u32[]{:S(2)}) copy-start(bf16[49,80,256]{2,1,0:T(8,128)(2,1)} %get-tuple-element.12.terms_ref) | copy-start | bytes 6021124
